TPU v7x, 512 devices: a whole 4x4x16 slice. The times are simulated.
512 devices in a mesh: pts: 64 (over y, z), tgt: 8 (over x, core).
Axes of the slice: x: 4, y: 4, z: 16, core: 2. Of those that a mesh axis runs over, the one named last changes fastest.
Arguments:
- template_points: float32 [3, 98304], P(None, 'pts'), may hold values from 0 to 24
- template_mass: float32 [98304], P('pts'), may hold values from 0.5 to 2
- target_points: float32 [32, 3, 98304], P('tgt', None, 'pts'), may hold values from 0 to 24
- target_mass: float32 [32, 98304], P('tgt', 'pts'), may hold values from 0.5 to 2
- pattern: int32 [32, 768, 4], P('tgt', 'pts'), may hold values from 0 to 767, as said below
Outputs:
- position_grad: float32 [3, 98304], P(None, 'pts')
- target_potentials: float32 [32, 98304], P('tgt', 'pts')
Inputs may be any that keep to these rules, and one draw needn't show every extreme that they name: pattern[t, p, 0] is p; the other 3 entries of pattern[t, p, :] are distinct, differ from p, and name target blocks q with |q - p| <= 12.
All inputs are finite; a program needn't handle non-finite values.
Results may differ from a plain program's by a relative error of at most 0.0003.
Values sent between devices are 32-bit elements; how exact they have to be, the bound alone decides.
A program may use at most 128 MiB of HBM per device.

v0:
```python
import jax
import jax.numpy as jnp
from jax import lax
from jax.sharding import PartitionSpec as P

BLOCK = 128
REACH = 12
ITERS = 3


entropic = 0.02
marginal = 0.5
lowest = -1e30


def shifted(value, axis, by):
    length = lax.axis_size(axis)
    pairs = [(i, i + by) for i in range(length) if 0 <= i + by < length]
    return lax.ppermute(value, axis, pairs)


def with_halo(cells, sides, width):
    for axis, dim in sides:
        count = lax.axis_size(axis)
        ends = count - 1
        head = lax.slice_in_dim(cells, 0, width, axis=dim)
        tail = lax.slice_in_dim(cells, cells.shape[dim] - width, cells.shape[dim], axis=dim)
        cells = jnp.concatenate(
            [
                lax.ppermute(tail, axis, [(i, (i + 1) % count) for i in range(ends)]),
                cells,
                lax.ppermute(head, axis, [((i + 1) % count, i) for i in range(ends)]),
            ],
            axis=dim,
        )
    return cells


def pair_costs(xb, coords):
    diff = xb[:, :, :, None, None] - coords[:, :, None, :, :]
    return 0.5 * jnp.sum(diff * diff, axis=1)


def template_update(cost, logb_pairs, g_pairs):
    shrink = marginal / (marginal + entropic)
    arg = logb_pairs[:, None] + (g_pairs[:, None] - cost) / entropic
    top = jnp.max(arg, axis=(2, 3))
    total = jnp.sum(jnp.exp(arg - top[:, :, None, None]), axis=(2, 3))
    return -shrink * entropic * (top + jnp.log(total))


def window_partials(cost, f_now, log_a, onehot, links):
    arg = log_a[:, :, None, None] + (f_now[:, :, None, None] - cost) / entropic
    block_max = jnp.max(arg, axis=1)
    block_sum = jnp.sum(jnp.exp(arg - block_max[:, None]), axis=1)
    win_max = jnp.max(
        jnp.where(onehot[..., None] > 0, block_max[:, :, None, :], lowest), axis=(0, 1)
    )
    scaled = block_sum * jnp.exp(block_max - win_max[links])
    win_sum = jnp.einsum("bkw,bkj->wj", onehot, scaled, precision=lax.Precision.HIGHEST)
    return (win_max, win_sum)


def position_term(xb, coords, cost, log_a, logb_pairs, f_now, g_pairs):
    plan = jnp.exp(
        log_a[:, :, None, None]
        + logb_pairs[:, None]
        + (f_now[:, :, None, None] + g_pairs[:, None] - cost) / entropic
    )
    rows = jnp.sum(plan, axis=(2, 3))
    pulled = jnp.einsum("bikj,bckj->bci", plan, coords, precision=lax.Precision.HIGHEST)
    return xb * rows[:, None, :] - pulled


def combine_terms(maxima, sums):
    top = jnp.max(maxima, axis=1)
    total = jnp.sum(sums * jnp.exp(maxima - top[:, None]), axis=1)
    shrink = marginal / (marginal + entropic)
    return (top, total, shrink)


def settle_owners(win_max, win_sum, group, blk, index, count):
    upper_part = jnp.stack([win_max[:, :REACH], win_sum[:, :REACH]], axis=1)
    lower_part = jnp.stack([win_max[:, blk + REACH :], win_sum[:, blk + REACH :]], axis=1)
    from_upper = shifted(upper_part, "pts", -1)
    from_lower = shifted(lower_part, "pts", 1)
    upper_ok = index < count - 1
    lower_ok = index > 0
    filler_max = jnp.full((group, blk - REACH, BLOCK), lowest, jnp.float32)
    filler_sum = jnp.zeros((group, blk - REACH, BLOCK), jnp.float32)
    upper_max = jnp.concatenate([filler_max, jnp.where(upper_ok, from_upper[:, 0], lowest)], axis=1)
    upper_sum = jnp.concatenate([filler_sum, jnp.where(upper_ok, from_upper[:, 1], 0.0)], axis=1)
    lower_max = jnp.concatenate([jnp.where(lower_ok, from_lower[:, 0], lowest), filler_max], axis=1)
    lower_sum = jnp.concatenate([jnp.where(lower_ok, from_lower[:, 1], 0.0), filler_sum], axis=1)
    maxima = jnp.stack([win_max[:, REACH : REACH + blk], upper_max, lower_max], axis=1)
    sums = jnp.stack([win_sum[:, REACH : REACH + blk], upper_sum, lower_sum], axis=1)
    top, total, shrink = combine_terms(maxima, sums)
    return -shrink * entropic * (top + jnp.log(total))


def shards(template_points, template_mass, target_points, target_mass, pattern):
    group, blk, pairs = pattern.shape
    span = blk + 2 * REACH
    width = blk * BLOCK
    index = lax.axis_index("pts")
    count = lax.axis_size("pts")
    links = pattern - (index * blk - REACH)
    xb = template_points.reshape(3, blk, BLOCK).transpose(1, 0, 2)
    log_a = jnp.log(template_mass).reshape(blk, BLOCK)
    log_b = jnp.log(target_mass)
    fixed = jnp.concatenate([target_points, log_b[:, None, :]], axis=1)
    beside_all = with_halo(fixed, (("pts", 2),), REACH * BLOCK)
    blocks = beside_all.reshape(group, 4, span, BLOCK).transpose(0, 2, 1, 3)
    picked = jax.vmap(lambda table, rows: table[rows])(blocks, links)
    coords = picked[:, :, :, :3].transpose(0, 1, 3, 2, 4)
    logb_pairs = picked[:, :, :, 3]
    cost = lax.map(lambda scan_coords: pair_costs(xb, scan_coords), coords)
    onehot = (links[..., None] == jnp.arange(span, dtype=jnp.int32)).astype(jnp.float32)
    g_window = jnp.zeros((group, span, BLOCK), jnp.float32)
    g_own = jnp.zeros((group, blk, BLOCK), jnp.float32)
    f_now = jnp.zeros((group, blk, BLOCK), jnp.float32)
    for turn in range(ITERS):
        g_pairs = jax.vmap(lambda table, rows: table[rows])(g_window, links)
        f_now = lax.map(
            lambda members: template_update(members[0], members[1], members[2]),
            (cost, logb_pairs, g_pairs),
        )
        win_max, win_sum = lax.map(
            lambda members: window_partials(members[0], members[1], log_a, members[2], members[3]),
            (cost, f_now, onehot, links),
        )
        g_own = settle_owners(win_max, win_sum, group, blk, index, count)
        g_window = with_halo(g_own.reshape(group, width), (("pts", 1),), REACH * BLOCK).reshape(
            group, span, BLOCK
        )
    g_pairs = jax.vmap(lambda table, rows: table[rows])(g_window, links)
    grads = lax.map(
        lambda members: position_term(
            xb, members[1], members[0], log_a, members[2], members[3], members[4]
        ),
        (cost, coords, logb_pairs, f_now, g_pairs),
    )
    local_grad = jnp.sum(grads, axis=0)
    summed = lax.psum(local_grad, "tgt")
    position_grad = summed.transpose(1, 0, 2).reshape(3, width)
    return (position_grad, g_own.reshape(group, width))


def solution(mesh):
    placed = (
        P(None, "pts"),
        P("pts"),
        P("tgt", None, "pts"),
        P("tgt", "pts"),
        P("tgt", "pts", None),
    )
    return jax.shard_map(
        shards,
        mesh=mesh,
        in_specs=placed,
        out_specs=(P(None, "pts"), P("tgt", "pts")),
        check_vma=False,
    )
```

profile of v0, /device:TPU:1, one launch (start us, length us, event | category | flops | bytes accessed | tf_op | source)
XLA Modules:
  0.0 705.3 jit_solution(1660849794587543811)
XLA Ops:
  15.6 14.7 %while.86 = (s32[]{:T(128)}, f32[4,12,128,4,128]{4,2,3,1,0:T(8,128)}, f32[12,3,128]{2,1,0:T(4,128)S(1)}, f32[4,12,3,4,128]{4,3,2,1,0:T(4,128)S(1)}, s32[]{:T(128)}) while((s32[]{:T(128)}, f32[4,12,128,4,128]{4,2,3,1,0:T(8,128)}, f32[12,3,128]{2,1,0:T(4,128)S(1)}, f32[4,12,3,4,128]{4,3,2,1,0:T(4,128)S(1)}, s32[]{:T(128)}) %tuple.213), condition=%wide.region_2.3_spmd, body=%wide.region_0.2_spmd.sunk | while | flops 7077890 | bytes 9677377 | solution.py:117
  30.3 16.3 %copy.143 = f32[4,12,128,4,128]{4,3,2,1,0:T(4,128)} copy(f32[4,12,128,4,128]{4,2,3,1,0:T(8,128)} %get-tuple-element.1097) | data formatting | bytes 25165824 | tf_op jit(solution)/shard_map/while | solution.py:124
  46.6 115.8 %while.87 = (s32[]{:T(128)}, f32[4,12,128]{2,1,0:T(8,128)S(1)}, f32[4,12,4,128]{3,2,1,0:T(4,128)S(1)}, f32[4,12,4,128]{3,2,1,0:T(4,128)S(1)}, f32[4,12,128,4,128]{4,3,2,1,0:T(4,128)}, /*index=5*/s32[]{:T(128)}) while((s32[]{:T(128)}, f32[4,12,128]{2,1,0:T(8,128)S(1)}, f32[4,12,4,128]{3,2,1,0:T(4,128)S(1)}, f32[4,12,4,128]{3,2,1,0:T(4,128)S(1)}, ...), condition=%wide.region_6.7_spmd, body=%wide.region_3.6_spmd.sunk | while | flops 7077890 | bytes 6531157 | solution.py:124
  52.0 23.6 %exponential_reduce_fusion.12 = f32[12,128]{1,0:T(8,128)S(1)} fusion(f32[4,12,128,4,128]{4,3,2,1,0:T(4,128)} %get-tuple-element.963, s32[]{:T(128)} %get-tuple-element.953, f32[12,128]{1,0:T(8,128)S(1)} %fusion.93, f32[12,4,128]{2,1,0:T(4,128)S(1)} %get-tuple-element.881, f32[12,4,128]{2,1,0:T(4,128)S(1)} %get-tuple-element.882), kind=kLoop, calls=%fused_computation.14.clone.1 | loop fusion | flops 3930624 | bytes 3207172 | tf_op jit(solution)/shard_map/while/body/eval_jaxpr/reduce_sum | solution.py:48
  80.9 23.6 %exponential_reduce_fusion.12 = f32[12,128]{1,0:T(8,128)S(1)} fusion(f32[4,12,128,4,128]{4,3,2,1,0:T(4,128)} %get-tuple-element.963, s32[]{:T(128)} %get-tuple-element.953, f32[12,128]{1,0:T(8,128)S(1)} %fusion.93, f32[12,4,128]{2,1,0:T(4,128)S(1)} %get-tuple-element.881, f32[12,4,128]{2,1,0:T(4,128)S(1)} %get-tuple-element.882), kind=kLoop, calls=%fused_computation.14.clone.1 | loop fusion | flops 3930624 | bytes 3207172 | tf_op jit(solution)/shard_map/while/body/eval_jaxpr/reduce_sum | solution.py:48
  109.9 23.6 %exponential_reduce_fusion.12 = f32[12,128]{1,0:T(8,128)S(1)} fusion(f32[4,12,128,4,128]{4,3,2,1,0:T(4,128)} %get-tuple-element.963, s32[]{:T(128)} %get-tuple-element.953, f32[12,128]{1,0:T(8,128)S(1)} %fusion.93, f32[12,4,128]{2,1,0:T(4,128)S(1)} %get-tuple-element.881, f32[12,4,128]{2,1,0:T(4,128)S(1)} %get-tuple-element.882), kind=kLoop, calls=%fused_computation.14.clone.1 | loop fusion | flops 3930624 | bytes 3207172 | tf_op jit(solution)/shard_map/while/body/eval_jaxpr/reduce_sum | solution.py:48
  138.9 23.6 %exponential_reduce_fusion.12 = f32[12,128]{1,0:T(8,128)S(1)} fusion(f32[4,12,128,4,128]{4,3,2,1,0:T(4,128)} %get-tuple-element.963, s32[]{:T(128)} %get-tuple-element.953, f32[12,128]{1,0:T(8,128)S(1)} %fusion.93, f32[12,4,128]{2,1,0:T(4,128)S(1)} %get-tuple-element.881, f32[12,4,128]{2,1,0:T(4,128)S(1)} %get-tuple-element.882), kind=kLoop, calls=%fused_computation.14.clone.1 | loop fusion | flops 3930624 | bytes 3207172 | tf_op jit(solution)/shard_map/while/body/eval_jaxpr/reduce_sum | solution.py:48
  162.5 62.3 %while.88 = (s32[]{:T(128)}, f32[4,36,128]{2,0,1:T(4,128)S(1)}, f32[4,36,128]{2,0,1:T(4,128)S(1)}, f32[4,12,4,36]{3,1,2,0:T(8,128)S(1)}, f32[1536]{0:T(1024)S(1)...) while((s32[]{:T(128)}, f32[4,36,128]{2,0,1:T(4,128)S(1)}, ...), condition=%wide.region_11.12_spmd, body=%wide.region_7.11_spmd.sunk | while | flops 10172754 | bytes 6835333 | solution.py:128
  162.5 6.7 fusion.96
  178.1 6.7 fusion.96
  246.1 115.9 %while.89 = (s32[]{:T(128)}, f32[4,12,128]{2,1,0:T(8,128)S(1)}, f32[4,12,4,128]{3,2,1,0:T(4,128)S(1)}, f32[4,12,4,128]{3,2,1,0:T(4,128)S(1)}, f32[4,12,128,4,128]{4,3,2,1,0:T(4,128)}, /*index=5*/s32[]{:T(128)}) while((s32[]{:T(128)}, f32[4,12,128]{2,1,0:T(8,128)S(1)}, f32[4,12,4,128]{3,2,1,0:T(4,128)S(1)}, ...), condition=%wide.region_16.17_spmd, body=%wide.region_13.16_spmd.sunk | while | flops 7077890 | bytes 6531157 | solution.py:124
  251.5 23.6 %exponential_reduce_fusion.14 = f32[12,128]{1,0:T(8,128)S(1)} fusion(f32[4,12,128,4,128]{4,3,2,1,0:T(4,128)} %get-tuple-element.1011, s32[]{:T(128)} %get-tuple-element.1001, f32[12,128]{1,0:T(8,128)S(1)} %fusion.97, f32[12,4,128]{2,1,0:T(4,128)S(1)} %get-tuple-element.896, f32[12,4,128]{2,1,0:T(4,128)S(1)} %get-tuple-element.897), kind=kLoop, calls=%fused_computation.22.clone.1 | loop fusion | flops 3930624 | bytes 3207172 | tf_op jit(solution)/shard_map/while/body/eval_jaxpr/reduce_sum | solution.py:48
  280.4 23.6 %exponential_reduce_fusion.14 = f32[12,128]{1,0:T(8,128)S(1)} fusion(f32[4,12,128,4,128]{4,3,2,1,0:T(4,128)} %get-tuple-element.1011, s32[]{:T(128)} %get-tuple-element.1001, f32[12,128]{1,0:T(8,128)S(1)} %fusion.97, f32[12,4,128]{2,1,0:T(4,128)S(1)} %get-tuple-element.896, f32[12,4,128]{2,1,0:T(4,128)S(1)} %get-tuple-element.897), kind=kLoop, calls=%fused_computation.22.clone.1 | loop fusion | flops 3930624 | bytes 3207172 | tf_op jit(solution)/shard_map/while/body/eval_jaxpr/reduce_sum | solution.py:48
  309.4 23.6 %exponential_reduce_fusion.14 = f32[12,128]{1,0:T(8,128)S(1)} fusion(f32[4,12,128,4,128]{4,3,2,1,0:T(4,128)} %get-tuple-element.1011, s32[]{:T(128)} %get-tuple-element.1001, f32[12,128]{1,0:T(8,128)S(1)} %fusion.97, f32[12,4,128]{2,1,0:T(4,128)S(1)} %get-tuple-element.896, f32[12,4,128]{2,1,0:T(4,128)S(1)} %get-tuple-element.897), kind=kLoop, calls=%fused_computation.22.clone.1 | loop fusion | flops 3930624 | bytes 3207172 | tf_op jit(solution)/shard_map/while/body/eval_jaxpr/reduce_sum | solution.py:48
  338.4 23.6 %exponential_reduce_fusion.14 = f32[12,128]{1,0:T(8,128)S(1)} fusion(f32[4,12,128,4,128]{4,3,2,1,0:T(4,128)} %get-tuple-element.1011, s32[]{:T(128)} %get-tuple-element.1001, f32[12,128]{1,0:T(8,128)S(1)} %fusion.97, f32[12,4,128]{2,1,0:T(4,128)S(1)} %get-tuple-element.896, f32[12,4,128]{2,1,0:T(4,128)S(1)} %get-tuple-element.897), kind=kLoop, calls=%fused_computation.22.clone.1 | loop fusion | flops 3930624 | bytes 3207172 | tf_op jit(solution)/shard_map/while/body/eval_jaxpr/reduce_sum | solution.py:48
  362.0 62.3 %while.90 = (s32[]{:T(128)}, f32[4,36,128]{2,0,1:T(4,128)S(1)}, f32[4,36,128]{2,0,1:T(4,128)S(1)}, f32[4,12,4,36]{3,1,2,0:T(8,128)S(1)}, f32[1536]{0:T(1024)S(1)...) while((s32[]{:T(128)}, f32[4,36,128]{2,0,1:T(4,128)S(1)}, ...), condition=%wide.region_21.22_spmd, body=%wide.region_17.21_spmd.sunk | while | flops 10172754 | bytes 6835333 | solution.py:128
  444.9 115.9 %while.91 = (s32[]{:T(128)}, f32[4,12,128]{2,1,0:T(8,128)S(1)}, f32[4,12,4,128]{3,2,1,0:T(4,128)S(1)}, f32[4,12,4,128]{3,2,1,0:T(4,128)S(1)}, f32[4,12,128,4,128]{4,3,2,1,0:T(4,128)}, /*index=5*/s32[]{:T(128)}) while((s32[]{:T(128)}, f32[4,12,128]{2,1,0:T(8,128)S(1)}, f32[4,12,4,128]{3,2,1,0:T(4,128)S(1)}, ...), condition=%wide.region_26.27_spmd, body=%wide.region_23.26_spmd.sunk | while | flops 7077890 | bytes 6531157 | solution.py:124
  450.3 23.6 %exponential_reduce_fusion.16 = f32[12,128]{1,0:T(8,128)S(1)} fusion(f32[4,12,128,4,128]{4,3,2,1,0:T(4,128)} %get-tuple-element.1059, s32[]{:T(128)} %get-tuple-element.1049, f32[12,128]{1,0:T(8,128)S(1)} %fusion.101, f32[12,4,128]{2,1,0:T(4,128)S(1)} %get-tuple-element.911, f32[12,4,128]{2,1,0:T(4,128)S(1)} %get-tuple-element.912), kind=kLoop, calls=%fused_computation.30.clone.1 | loop fusion | flops 3930624 | bytes 3207172 | tf_op jit(solution)/shard_map/while/body/eval_jaxpr/reduce_sum | solution.py:48
  479.3 23.6 %exponential_reduce_fusion.16 = f32[12,128]{1,0:T(8,128)S(1)} fusion(f32[4,12,128,4,128]{4,3,2,1,0:T(4,128)} %get-tuple-element.1059, s32[]{:T(128)} %get-tuple-element.1049, f32[12,128]{1,0:T(8,128)S(1)} %fusion.101, f32[12,4,128]{2,1,0:T(4,128)S(1)} %get-tuple-element.911, f32[12,4,128]{2,1,0:T(4,128)S(1)} %get-tuple-element.912), kind=kLoop, calls=%fused_computation.30.clone.1 | loop fusion | flops 3930624 | bytes 3207172 | tf_op jit(solution)/shard_map/while/body/eval_jaxpr/reduce_sum | solution.py:48
  508.3 23.6 %exponential_reduce_fusion.16 = f32[12,128]{1,0:T(8,128)S(1)} fusion(f32[4,12,128,4,128]{4,3,2,1,0:T(4,128)} %get-tuple-element.1059, s32[]{:T(128)} %get-tuple-element.1049, f32[12,128]{1,0:T(8,128)S(1)} %fusion.101, f32[12,4,128]{2,1,0:T(4,128)S(1)} %get-tuple-element.911, f32[12,4,128]{2,1,0:T(4,128)S(1)} %get-tuple-element.912), kind=kLoop, calls=%fused_computation.30.clone.1 | loop fusion | flops 3930624 | bytes 3207172 | tf_op jit(solution)/shard_map/while/body/eval_jaxpr/reduce_sum | solution.py:48
  537.2 23.6 %exponential_reduce_fusion.16 = f32[12,128]{1,0:T(8,128)S(1)} fusion(f32[4,12,128,4,128]{4,3,2,1,0:T(4,128)} %get-tuple-element.1059, s32[]{:T(128)} %get-tuple-element.1049, f32[12,128]{1,0:T(8,128)S(1)} %fusion.101, f32[12,4,128]{2,1,0:T(4,128)S(1)} %get-tuple-element.911, f32[12,4,128]{2,1,0:T(4,128)S(1)} %get-tuple-element.912), kind=kLoop, calls=%fused_computation.30.clone.1 | loop fusion | flops 3930624 | bytes 3207172 | tf_op jit(solution)/shard_map/while/body/eval_jaxpr/reduce_sum | solution.py:48
  560.8 62.3 %while.92 = (s32[]{:T(128)}, f32[4,36,128]{2,0,1:T(4,128)S(1)}, f32[4,36,128]{2,0,1:T(4,128)S(1)}, f32[4,12,4,36]{3,1,2,0:T(8,128)S(1)}, f32[1536]{0:T(1024)S(1)...) while((s32[]{:T(128)}, f32[4,36,128]{2,0,1:T(4,128)S(1)}, ...), condition=%wide.region_31.32_spmd, body=%wide.region_27.31_spmd.sunk | while | flops 10172754 | bytes 6835333 | solution.py:128
  643.4 31.7 %while.93 = (s32[]{:T(128)}, f32[4,12,3,128]{3,2,1,0:T(4,128)S(1)}, f32[1536]{0:T(1024)S(1)}, f32[4,12,4,128]{3,2,1,0:T(4,128)S(1)}, f32[4,12,128]{2,1,0:T(8,128...) while((s32[]{:T(128)}, f32[4,12,3,128]{3,2,1,0:T(4,128)S(1)}, ...), condition=%wide.region_35.36_spmd, body=%wide.region_33.35_spmd.sunk | while | flops 36969984 | bytes 6692465 | solution.py:137
  675.2 29.9 %psum.7 = f32[3,1536]{1,0:T(4,128)} all-reduce(f32[3,1536]{1,0:T(4,128)S(1)} %bitcast.497), channel_id=1, replica_groups=mesh['pts'=64,'tgt'=8] {'tgt'}, use_global_device_ids=true, to_apply=%region_37.38 | all-reduce | flops 4608 | bytes 36864 | tf_op jit(solution)/shard_map/psum | solution.py:144
  (354 shorter events, 359.3 us)
Async XLA Ops:
  0.6 15.0 %copy-start = (f32[3,1536]{1,0:T(4,128)S(1)}, f32[3,1536]{1,0:T(4,128)}, u32[]{:S(2)}) copy-start(f32[3,1536]{1,0:T(4,128)} %param.21) | copy-start | bytes 55300
  2.3 9.3 %collective-permute-start = (f32[4,4,1536]{2,0,1:T(4,128)S(1)}, f32[4,4,1536]{2,0,1:T(4,128)S(1)}, u32[]{:S(2)}, u32[]{:S(2)}) collective-permute-start(f32[4,4,1536]{2,0,1:T(4,128)S(1)} %pad_maximum_fusion.1), channel_id=1, source_target_pairs={{0,8},{8,16},{16,24},{24,32},{32,40},{40,48},{48,56},{56,64},{64,7... | collective-permute-start | bytes 294920 | tf_op jit(solution)/shard_map/ppermute | solution.py:30
  6.7 5.5 collective-permute-start.1
  224.9 5.2 collective-permute-start.3
  228.7 5.9 collective-permute-start.2
  234.8 6.4 collective-permute-start.4
  239.4 4.8 collective-permute-start.5
  424.4 5.9 collective-permute-start.7
  429.0 4.8 collective-permute-start.6
  433.9 5.7 collective-permute-start.8
  438.1 4.9 collective-permute-start.9
  623.2 5.6 collective-permute-start.11
  627.5 4.8 collective-permute-start.10
  632.5 11.0 %copy-start.1 = (f32[4,1536]{1,0:T(4,128)}, f32[4,1536]{1,0:T(4,128)S(1)}, u32[]{:S(2)}) copy-start(f32[4,1536]{1,0:T(4,128)S(1)} %fusion.66) | copy-start | bytes 73732
  632.5 6.0 collective-permute-start.12
  636.9 4.6 collective-permute-start.13
where the time goes:
time: 718 us; the launch traced here: 705 us
  other arithmetic  544 us (76%)
  local copies, waits for them, and re-layouts  42.9 us (6%)
  starting transfers between devices  40.2 us (6%)
  blocking collectives  29.9 us (4%)
  matrix products  23.5 us (3%)
  waiting for transfers between devices  21.6 us (3%)
    reduce_sum x12, other arithmetic, template_update(): total = jnp.sum(jnp.exp(arg - top[:, :, None, None]), axis=(2, 3))  283 us
    reduce_max x12, other arithmetic, window_partials(): block_max = jnp.max(arg, axis=1)  80.2 us
    reduce_sum x12, other arithmetic, window_partials(): block_sum = jnp.sum(jnp.exp(arg - block_max[:, None]), axis=1)  79.9 us
    reduce_max x12, other arithmetic, template_update(): top = jnp.max(arg, axis=(2, 3))  64 us
    psum x1, blocking collectives, shards(): summed = lax.psum(local_grad, 'tgt')  29.9 us
    dot_general x4, matrix products, position_term(): jnp.einsum('bikj,bckj->bci', plan, coords, precision=lax.Precision.HIGHEST)  20.7 us
    ppermute x4, starting transfers between devices, with_halo(): lax.ppermute(tail, axis, [(i, (i + 1) % count) for i in range(ends)])  17.5 us
    ppermute x6, starting transfers between devices, shifted(): return lax.ppermute(value, axis, pairs)  16.6 us
  transfers between devices with their start and end apart: 14, of which 7 were waited for; matrix products, arithmetic and copies ran while one was open for 1% of the time, Pallas kernels for 0%

commit v1 on v0

v1 whole, which is shorter than its diff:
```python
import functools
import math

import jax
import jax.numpy as jnp
from jax import lax
from jax.experimental import pallas as pl
from jax.experimental.pallas import tpu as pltpu
from jax.sharding import PartitionSpec as P

BLOCK = 128
REACH = 12
ITERS = 3

entropic = 0.02
marginal = 0.5
lowest = -1e30
shrink = marginal / (marginal + entropic)
unit = math.log2(math.e) / entropic

MESH = pl.DeviceIdType.MESH
ROWS = 16
SPAN = 3 * ROWS
OWN = slice(ROWS, 2 * ROWS)


def kernel(group, blk, pairs, count, peers, refs, outs, scratch):
    xp_ref, xm_ref, yp_ref, ym_ref, links_ref = refs
    grad_ref, pot_ref = outs
    s = scratch
    me = lax.axis_index("pts")
    mine = lax.axis_index("tgt")
    upper = lax.rem(me + 1, count)
    lower = lax.rem(me + count - 1, count)
    base = me * blk

    barrier = pltpu.get_barrier_semaphore()
    for side in (lower, upper):
        pl.semaphore_signal(barrier, inc=1, device_id={"pts": side}, device_id_type=MESH)
    for step in range(1, peers):
        pl.semaphore_signal(
            barrier, inc=1, device_id={"tgt": lax.rem(mine + step, peers)}, device_id_type=MESH
        )

    def both_ways(src_lower, src_upper, dst_lower, dst_upper, send, recv):
        down = pltpu.make_async_remote_copy(
            src_ref=src_lower, dst_ref=dst_upper, send_sem=send.at[0], recv_sem=recv.at[1],
            device_id={"pts": lower}, device_id_type=MESH,
        )
        up = pltpu.make_async_remote_copy(
            src_ref=src_upper, dst_ref=dst_lower, send_sem=send.at[1], recv_sem=recv.at[0],
            device_id={"pts": upper}, device_id_type=MESH,
        )
        return down, up

    def coord_copies(t):
        win = s["coord"][t]
        own = win.at[:, pl.ds(ROWS, ROWS)]
        return both_ways(
            own, own, win.at[:, pl.ds(0, ROWS)], win.at[:, pl.ds(2 * ROWS, ROWS)],
            s["c_send"].at[t], s["c_recv"].at[t],
        )

    def dual_copies(t):
        win = s["dual"][t]
        own = win.at[pl.ds(ROWS, ROWS)]
        return both_ways(
            own, own, win.at[pl.ds(0, ROWS)], win.at[pl.ds(2 * ROWS, ROWS)],
            s["d_send"].at[t], s["d_recv"].at[t],
        )

    def part_copies(t):
        win = s["part"].at[t]
        return both_ways(
            win.at[pl.ds(0, ROWS)], win.at[pl.ds(2 * ROWS, ROWS)],
            s["got"].at[t, 0], s["got"].at[t, 1],
            s["p_send"].at[t], s["p_recv"].at[t],
        )

    def start(copies):
        for c in copies:
            c.start()

    def wait_send(copies):
        for c in copies:
            c.wait_send()

    def wait_recv(copies):
        for c in copies:
            c.wait_recv()

    for t in range(group):
        for c in range(3):
            s["coord"][t][c, OWN] = jnp.zeros((ROWS, BLOCK), jnp.float32)
            for q in range(blk):
                s["coord"][t][c, ROWS + q : ROWS + q + 1] = yp_ref[t, c : c + 1, q * BLOCK : (q + 1) * BLOCK]
        s["logb"][t] = jnp.zeros((ROWS, BLOCK), jnp.float32)
        for q in range(blk):
            s["logb"][t, q : q + 1] = jnp.log2(ym_ref[t : t + 1, q * BLOCK : (q + 1) * BLOCK])
        s["dual"][t][OWN] = s["logb"][t]

    pl.semaphore_wait(barrier, 2 + peers - 1)
    for t in range(group):
        start(coord_copies(t))
        start(dual_copies(t))

    def columns(p, _):
        lanes = pl.ds(pl.multiple_of(p * BLOCK, BLOCK), BLOCK)
        for c in range(3):
            row = xp_ref[c : c + 1, lanes]
            s["xcol"][c, p] = jnp.transpose(jnp.broadcast_to(row, (BLOCK, BLOCK)))
        row = jnp.log2(xm_ref[:, lanes])
        s["acol"][p] = jnp.transpose(jnp.broadcast_to(row, (BLOCK, BLOCK)))
        return 0

    lax.fori_loop(0, blk, columns, 0)

    rows_iota = lax.broadcasted_iota(jnp.int32, (SPAN, BLOCK), 0)

    def window_row(t, p, k):
        w = jnp.clip(links_ref[t, p, k] - base + REACH, 0, blk + 2 * REACH - 1)
        pad = ROWS - blk
        return w + jnp.where(w >= blk, pad, 0) + jnp.where(w >= 2 * blk, pad, 0)

    def sweep(t, first, last):
        cost = s["cost"]

        def body(p, _):
            where = [ROWS + p] + [window_row(t, p, k) for k in range(1, pairs)]
            duals = [s["dual"][t][pl.ds(w, 1), :] for w in where]
            if first:
                for k in range(pairs):
                    y = [s["coord"][t][c, pl.ds(where[k], 1), :] for c in range(3)]
                    for r in range(0, BLOCK, 32):
                        d = [s["xcol"][c, p, r : r + 32] - y[c] for c in range(3)]
                        total = d[0] * d[0] + d[1] * d[1] + d[2] * d[2]
                        cost[t, p, k, r : r + 32] = total * (0.5 * unit)
            heads = []
            for r in range(0, BLOCK, 32):
                args = [duals[k] - cost[t, p, k, r : r + 32] for k in range(pairs)]
                top = functools.reduce(jnp.maximum, args)
                top = jnp.max(top, axis=1, keepdims=True)
                total = functools.reduce(jnp.add, [jnp.exp2(a - top) for a in args])
                total = jnp.sum(total, axis=1, keepdims=True)
                f = (top + jnp.log2(total)) * (-shrink)
                heads.append(s["acol"][p, r : r + 32] + f)
            head = jnp.concatenate(heads, axis=0)
            terms = []
            for k in range(pairs):
                arg = head - cost[t, p, k]
                top = jnp.max(arg, axis=0, keepdims=True)
                h = jnp.exp2(arg - top)
                if last:
                    cost[t, p, k] = h
                    s["tops"][t, p, k : k + 1] = top
                terms.append(top + jnp.log2(jnp.sum(h, axis=0, keepdims=True)))
            picked = jnp.where(rows_iota == where[0], terms[0], lowest)
            for k in range(1, pairs):
                picked = jnp.where(rows_iota == where[k], terms[k], picked)
            s["picked"][p] = picked
            s["best"][...] = jnp.maximum(s["best"][...], picked)
            return 0

        s["best"][...] = jnp.full((SPAN, BLOCK), lowest, jnp.float32)
        lax.fori_loop(0, blk, body, 0)
        best = s["best"][...]

        def add(p, total):
            return total + jnp.exp2(s["picked"][p] - best)

        total = lax.fori_loop(0, blk, add, jnp.zeros((SPAN, BLOCK), jnp.float32), unroll=True)
        if not first:
            wait_send(part_copies(t))
        s["part"][t] = best + jnp.log2(total)
        start(part_copies(t))

    def settle(t):
        wait_recv(part_copies(t))
        own = s["part"][t, OWN]
        sides = [s["got"][t, 0], s["got"][t, 1]]
        top = jnp.maximum(jnp.maximum(own, sides[0]), sides[1])
        total = jnp.exp2(own - top) + jnp.exp2(sides[0] - top) + jnp.exp2(sides[1] - top)
        g = (top + jnp.log2(total)) * (-shrink)
        wait_send(dual_copies(t))
        s["dual"][t][OWN] = s["logb"][t] + g
        start(dual_copies(t))
        return g

    def pull(t, first):
        acc = s["acc"]

        def body(p, _):
            where = [ROWS + p] + [window_row(t, p, k) for k in range(1, pairs)]
            scale, y = [], []
            for k in range(pairs):
                scale.append(jnp.exp2(s["tops"][t, p, k : k + 1] + s["dual"][t][pl.ds(where[k], 1), :]))
                y.append([s["coord"][t][c, pl.ds(where[k], 1), :] for c in range(3)])
            for r in range(0, BLOCK, 32):
                sums = [None] * 4 if first else [acc[p, c, r : r + 32] for c in range(4)]
                for k in range(pairs):
                    plan = s["cost"][t, p, k, r : r + 32] * scale[k]
                    new = [plan * y[k][c] for c in range(3)] + [plan]
                    sums = [b if a is None else a + b for a, b in zip(sums, new)]
                for c in range(4):
                    acc[p, c, r : r + 32] = sums[c]
            return 0

        lax.fori_loop(0, blk, body, 0)

    steps = [(turn, t) for turn in range(ITERS) for t in range(group)]
    for at, (turn, t) in enumerate(steps):
        if turn == 0:
            wait_recv(coord_copies(t))
        wait_recv(dual_copies(t))
        sweep(t, turn == 0, turn == ITERS - 1)
        if at:
            before, u = steps[at - 1]
            g = settle(u)
            if before == ITERS - 1:
                pot_ref[u] = g * (1.0 / unit)

    wait_recv(dual_copies(0))
    pull(0, True)
    pot_ref[group - 1] = settle(group - 1) * (1.0 / unit)
    for t in range(1, group):
        wait_recv(dual_copies(t))
        pull(t, False)

    s["grads"][mine] = jnp.zeros(s["grads"].shape[1:], jnp.float32)

    def finish(p, _):
        rows = s["acc"][p, 3]
        for c in range(3):
            part = s["xcol"][c, p] * rows - s["acc"][p, c]
            s["grads"][mine, pl.ds(c * ROWS + p, 1), :] = jnp.sum(jnp.transpose(part), axis=0, keepdims=True)
        return 0

    lax.fori_loop(0, blk, finish, 0)

    def grad_copy(to, slot):
        return pltpu.make_async_remote_copy(
            src_ref=s["grads"].at[mine], dst_ref=s["grads"].at[slot],
            send_sem=s["g_send"].at[to], recv_sem=s["g_recv"].at[slot],
            device_id={"tgt": to}, device_id_type=MESH,
        )

    others = [lax.rem(mine + step, peers) for step in range(1, peers)]
    for q in others:
        grad_copy(q, mine).start()
    for t in range(group):
        wait_send(coord_copies(t))
        wait_send(dual_copies(t))
        wait_send(part_copies(t))
    for q in others:
        grad_copy(q, q).wait_recv()
    total = s["grads"][0]
    for q in range(1, peers):
        total = total + s["grads"][q]
    for c in range(3):
        grad_ref[c] = total[c * ROWS : (c + 1) * ROWS]
    for q in others:
        grad_copy(q, mine).wait_send()


def shards(template_points, template_mass, target_points, target_mass, pattern):
    group, blk, pairs = pattern.shape
    width = blk * BLOCK
    count = lax.axis_size("pts")
    peers = lax.axis_size("tgt")
    f32 = jnp.float32

    names = {
        "coord": [pltpu.VMEM((3, SPAN, BLOCK), f32) for _ in range(group)],
        "dual": [pltpu.VMEM((SPAN, BLOCK), f32) for _ in range(group)],
        "logb": pltpu.VMEM((group, ROWS, BLOCK), f32),
        "part": pltpu.VMEM((group, SPAN, BLOCK), f32),
        "got": pltpu.VMEM((group, 2, ROWS, BLOCK), f32),
        "cost": pltpu.VMEM((group, blk, pairs, BLOCK, BLOCK), f32),
        "xcol": pltpu.VMEM((3, blk, BLOCK, BLOCK), f32),
        "acol": pltpu.VMEM((blk, BLOCK, BLOCK), f32),
        "tops": pltpu.VMEM((group, blk, 8, BLOCK), f32),
        "picked": pltpu.VMEM((blk, SPAN, BLOCK), f32),
        "best": pltpu.VMEM((SPAN, BLOCK), f32),
        "acc": pltpu.VMEM((blk, 4, BLOCK, BLOCK), f32),
        "grads": pltpu.VMEM((peers, SPAN, BLOCK), f32),
        "c_send": pltpu.SemaphoreType.DMA((group, 2)),
        "c_recv": pltpu.SemaphoreType.DMA((group, 2)),
        "d_send": pltpu.SemaphoreType.DMA((group, 2)),
        "d_recv": pltpu.SemaphoreType.DMA((group, 2)),
        "p_send": pltpu.SemaphoreType.DMA((group, 2)),
        "p_recv": pltpu.SemaphoreType.DMA((group, 2)),
        "g_send": pltpu.SemaphoreType.DMA((peers,)),
        "g_recv": pltpu.SemaphoreType.DMA((peers,)),
    }
    flat, tree = jax.tree.flatten(names)

    def run(*refs):
        kernel(group, blk, pairs, count, peers, refs[:5], refs[5:7], jax.tree.unflatten(tree, refs[7:]))

    whole = pl.BlockSpec(memory_space=pltpu.VMEM)
    elements = group * blk * pairs * BLOCK * BLOCK
    grad, pots = pl.pallas_call(
        run,
        out_shape=(
            jax.ShapeDtypeStruct((3, ROWS, BLOCK), f32),
            jax.ShapeDtypeStruct((group, ROWS, BLOCK), f32),
        ),
        in_specs=[whole, whole, whole, whole, pl.BlockSpec(memory_space=pltpu.SMEM)],
        out_specs=(whole, whole),
        scratch_shapes=flat,
        compiler_params=pltpu.CompilerParams(
            collective_id=0, has_side_effects=True, vmem_limit_bytes=48 * 1024 * 1024
        ),
        cost_estimate=pl.CostEstimate(
            flops=40 * elements, bytes_accessed=200000, transcendentals=6 * elements
        ),
        name="sinkhorn",
    )(template_points, template_mass.reshape(1, width), target_points, target_mass, pattern)
    return grad[:, :blk].reshape(3, width), pots[:, :blk].reshape(group, width)


def solution(mesh):
    placed = (
        P(None, "pts"),
        P("pts"),
        P("tgt", None, "pts"),
        P("tgt", "pts"),
        P("tgt", "pts", None),
    )
    return jax.shard_map(
        shards,
        mesh=mesh,
        in_specs=placed,
        out_specs=(P(None, "pts"), P("tgt", "pts")),
        check_vma=False,
    )
```

time: 718 us -> 89.5 us (0.12); the launches traced: 705 us -> 89.3 us
  other arithmetic: 544 us -> 0 us
  Pallas kernels: 0 us -> 85.6 us
  starting transfers between devices: 40.2 us -> 0 us
  local copies, waits for them, and re-layouts: 42.9 us -> 3.02 us
  blocking collectives: 29.9 us -> 0 us
  matrix products: 23.5 us -> 0 us
  waiting for transfers between devices: 21.6 us -> 0 us
    reduce_sum x36 -> x0, other arithmetic: 380 us -> none  [the longest x12 283 us: template_update(): total = jnp.sum(jnp.exp(arg - top[:, :, None, None]), axis=(2, 3))]
    reduce_max x36 -> x0, other arithmetic: 152 us -> none  [the longest x12 80.2 us: window_partials(): block_max = jnp.max(arg, axis=1)]
    pallas_call x0 -> x1, Pallas kernels: none -> 85.6 us  [shards(): pl.pallas_call(run, out_shape=(jax.ShapeDtypeStruct((3, ROWS, BLOCK), f32...]
    ppermute x14 -> x0, starting transfers between devices: 40.2 us -> none  [the longest x4 17.5 us: with_halo(): lax.ppermute(tail, axis, [(i, (i + 1) % count) for i in range(ends)])]
    psum x1 -> x0, blocking collectives: 29.9 us -> none  [shards(): summed = lax.psum(local_grad, 'tgt')]
    dot_general x16 -> x0, matrix products: 23.5 us -> none  [the longest x4 20.7 us: position_term(): jnp.einsum('bikj,bckj->bci', plan, coords, precision=lax.Precision.HIGHEST)]
    ppermute x14 -> x0, waiting for transfers between devices: 21.6 us -> none  [the longest x6 11.7 us: shifted(): return lax.ppermute(value, axis, pairs)]
    gather x19 -> x0, local copies, waits for them, and re-layouts: 16.5 us -> none  [the longest x4 7.48 us: shards(): g_pairs = jax.vmap(lambda table, rows: table[rows])(g_window, links)]
  transfers between devices with their start and end apart: 14 -> 0, of which waited for: 7 -> 0; matrix products, arithmetic and copies ran while one was open for 1% -> 0% of each run, Pallas kernels for 0% -> 0%
where the time goes in v1:
time: 89.5 us; the launch traced here: 89.3 us
  Pallas kernels  85.6 us (96%)
  local copies, waits for them, and re-layouts  3.02 us (3%)
    pallas_call x1, Pallas kernels, shards(): pl.pallas_call(run, out_shape=(jax.ShapeDtypeStruct((3, ROWS, BLOCK), f32...  85.6 us
    unnamed x12, local copies, waits for them, and re-layouts  2.31 us

profile of v1, /device:TPU:1, one launch (start us, length us, event | category | flops | bytes accessed | tf_op | source)
XLA Modules:
  0.0 89.3 jit_solution(9891912213237965835)
XLA Ops:
  0.6 0.0 copy-start.2
  0.6 0.7 reshape.13.refs_1_
  1.3 0.0 copy-done.2
  1.4 0.1 copy.10.refs_4_
  1.5 0.0 copy-start
  1.5 0.0 copy-start.1
  1.5 0.9 %copy.9.refs_2_ = f32[4,3,1536]{2,1,0:T(4,128)S(1)} copy(f32[4,3,1536]{2,0,1:T(4,128)} %param.7) | data formatting | bytes 147456 | tf_op args[2]
  2.4 0.0 copy-done
  2.4 0.0 copy-done.1
  2.4 85.6 %sinkhorn.1 = (f32[3,16,128]{2,1,0:T(8,128)S(1)}, f32[4,16,128]{2,1,0:T(8,128)S(1)}) custom-call(f32[3,1536]{1,0:T(4,128)S(1)} %copy-done, f32[1,1536]{1,0:T(1,128)S(1)} %reshape.13.refs_1_, f32[4,3,1536]{2,1,0:T(4,128)S(1)} %copy.9.refs_2_, f32[4,1536]{1,0:T(4,128)S(1)} %copy-done.1, s32[4,12,4]{2,1,0:T(8,128)S(1)} %copy.10.refs_4_), custom_call_target="tpu_custom_call" | custom-call | flops 125829120 | bytes 200000 | tf_op jit(solution)/shard_map/sinkhorn/pallas_call | solution.py:302
  88.1 0.6 copy.16
  88.7 0.6 copy.15
  (2 shorter events, 0.0 us)
Async XLA Ops:
  0.6 0.7 copy-start.2
  1.5 1.0 %copy-start = (f32[3,1536]{1,0:T(4,128)S(1)}, f32[3,1536]{1,0:T(4,128)}, u32[]{:S(2)}) copy-start(f32[3,1536]{1,0:T(4,128)} %refs_0_.1) | copy-start | bytes 55300
  1.5 1.0 %copy-start.1 = (f32[4,1536]{1,0:T(4,128)S(1)}, f32[4,1536]{1,0:T(4,128)}, u32[]{:S(2)}) copy-start(f32[4,1536]{1,0:T(4,128)} %refs_3_.1) | copy-start | bytes 73732

commit v2 on v1

v2 whole, which is shorter than its diff:
```python
import functools
import math

import jax
import jax.numpy as jnp
from jax import lax
from jax.experimental import pallas as pl
from jax.experimental.pallas import tpu as pltpu
from jax.sharding import PartitionSpec as P

BLOCK = 128
REACH = 12
ITERS = 3

entropic = 0.02
marginal = 0.5
lowest = -1e30
shrink = marginal / (marginal + entropic)
unit = math.log2(math.e) / entropic

MESH = pl.DeviceIdType.MESH
ROWS = 16
SPAN = 3 * ROWS
OWN = slice(ROWS, 2 * ROWS)
CORES = 2


def kernel(group, blk, pairs, count, peers, refs, outs, scratch):
    xp_ref, xm_ref, yp_ref, ym_ref, links_ref = refs
    grad_ref, pot_ref = outs
    s = scratch
    me = lax.axis_index("pts")
    mine = lax.axis_index("tgt")
    chips = peers // CORES
    chip = mine // CORES
    base = me * blk

    def at_distance(step):
        return {"pts": lax.rem(me + count + step, count)}

    sibling = {"tgt": chip * CORES + 1 - lax.rem(mine, CORES)}

    def same_core(step):
        return {"tgt": lax.rem(mine + step * CORES, peers)}

    greeted = [at_distance(step) for step in (-2, -1, 1, 2)]
    greeted += [sibling] + [same_core(step) for step in range(1, chips)]
    barrier = pltpu.get_barrier_semaphore()
    for other in greeted:
        pl.semaphore_signal(barrier, inc=1, device_id=other, device_id_type=MESH)

    def remote(src, dst, send, recv, to):
        return pltpu.make_async_remote_copy(
            src_ref=src, dst_ref=dst, send_sem=send, recv_sem=recv, device_id=to, device_id_type=MESH
        )

    def coord_copies(t):
        win, send, recv = s["coord"][t], s["c_send"].at[t], s["c_recv"].at[t]
        own = win.at[:, pl.ds(ROWS, ROWS)]
        return [
            remote(own, win.at[:, pl.ds(2 * ROWS, ROWS)], send.at[0], recv.at[0], at_distance(-1)),
            remote(own, win.at[:, pl.ds(0, ROWS)], send.at[1], recv.at[1], at_distance(1)),
        ]

    def part_copies(turn, t):
        part, got = s["part"].at[turn, t], s["got"].at[turn, t]
        send, recv = s["p_send"].at[turn, t], s["p_recv"].at[turn, t]
        lower, upper = pl.ds(0, ROWS), pl.ds(2 * ROWS, ROWS)
        not_lower, not_upper = pl.ds(ROWS, 2 * ROWS), pl.ds(0, 2 * ROWS)
        return [
            remote(part.at[lower], got.at[0, upper], send.at[0], recv.at[0], at_distance(-2)),
            remote(part.at[upper], got.at[1, lower], send.at[1], recv.at[1], at_distance(2)),
            remote(part.at[not_upper], got.at[1, not_lower], send.at[2], recv.at[2], at_distance(-1)),
            remote(part.at[not_lower], got.at[0, not_upper], send.at[3], recv.at[3], at_distance(1)),
        ]

    def start(copies):
        for c in copies:
            c.start()

    def wait_send(copies):
        for c in copies:
            c.wait_send()

    def wait_recv(copies):
        for c in copies:
            c.wait_recv()

    for t in range(group):
        for q in range(blk):
            lanes = slice(q * BLOCK, (q + 1) * BLOCK)
            for c in range(3):
                s["coord"][t][c, ROWS + q : ROWS + q + 1] = yp_ref[c, t : t + 1, lanes]
            s["coord"][t][3, ROWS + q : ROWS + q + 1] = jnp.log2(ym_ref[t : t + 1, lanes])
        for c in range(4):
            s["coord"][t][c, ROWS + blk : 2 * ROWS] = jnp.zeros((ROWS - blk, BLOCK), jnp.float32)

    pl.semaphore_wait(barrier, len(greeted))
    for t in range(group):
        start(coord_copies(t))

    def columns(p, _):
        lanes = pl.ds(pl.multiple_of(p * BLOCK, BLOCK), BLOCK)
        for c in range(3):
            row = xp_ref[c : c + 1, lanes]
            s["xcol"][c, p] = jnp.transpose(jnp.broadcast_to(row, (BLOCK, BLOCK)))
        row = jnp.log2(xm_ref[:, lanes])
        s["acol"][p] = jnp.transpose(jnp.broadcast_to(row, (BLOCK, BLOCK)))
        return 0

    lax.fori_loop(0, blk, columns, 0, unroll=2)

    rows_iota = lax.broadcasted_iota(jnp.int32, (SPAN, BLOCK), 0)

    def window_row(t, p, k):
        if k == 0:
            return ROWS + p
        w = jnp.clip(links_ref[t, k, p] - base + REACH, 0, blk + 2 * REACH - 1)
        pad = ROWS - blk
        return w + jnp.where(w >= blk, pad, 0) + jnp.where(w >= 2 * blk, pad, 0)

    def sweep(turn, t):
        first, last = turn == 0, turn == ITERS - 1
        cost = s["cost"]

        def body(p, _):
            where = [window_row(t, p, k) for k in range(pairs)]
            if first:
                duals = [s["coord"][t][3, pl.ds(w, 1), :] for w in where]
                for k in range(pairs):
                    y = [s["coord"][t][c, pl.ds(where[k], 1), :] for c in range(3)]
                    for r in range(0, BLOCK, 32):
                        d = [s["xcol"][c, p, r : r + 32] - y[c] for c in range(3)]
                        total = d[0] * d[0] + d[1] * d[1] + d[2] * d[2]
                        cost[t, p, k, r : r + 32] = total * (0.5 * unit)
            else:
                duals = [s["dual"][t, pl.ds(w, 1), :] for w in where]
            heads = []
            for r in range(0, BLOCK, 32):
                args = [duals[k] - cost[t, p, k, r : r + 32] for k in range(pairs)]
                top = functools.reduce(jnp.maximum, args)
                top = jnp.max(top, axis=1, keepdims=True)
                total = functools.reduce(jnp.add, [jnp.exp2(a - top) for a in args])
                total = jnp.sum(total, axis=1, keepdims=True)
                f = (top + jnp.log2(total)) * (-shrink)
                heads.append(s["acol"][p, r : r + 32] + f)
            head = jnp.concatenate(heads, axis=0)
            terms = []
            for k in range(pairs):
                arg = head - cost[t, p, k]
                top = jnp.max(arg, axis=0, keepdims=True)
                h = jnp.exp2(arg - top)
                if last:
                    cost[t, p, k] = h
                    s["tops"][t, p, k : k + 1] = top
                terms.append(top + jnp.log2(jnp.sum(h, axis=0, keepdims=True)))
            picked = jnp.where(rows_iota == where[0], terms[0], lowest)
            for k in range(1, pairs):
                picked = jnp.where(rows_iota == where[k], terms[k], picked)
            s["picked"][p] = picked
            s["best"][...] = jnp.maximum(s["best"][...], picked)
            return 0

        s["best"][...] = jnp.full((SPAN, BLOCK), lowest, jnp.float32)
        lax.fori_loop(0, blk, body, 0, unroll=4)
        best = s["best"][...]

        def add(p, total):
            return total + jnp.exp2(s["picked"][p] - best)

        total = lax.fori_loop(0, blk, add, jnp.zeros((SPAN, BLOCK), jnp.float32), unroll=True)
        s["part"][turn, t] = best + jnp.log2(total)
        start(part_copies(turn, t))

    def settle(turn, t):
        wait_recv(part_copies(turn, t))
        terms = [s["part"][turn, t], s["got"][turn, t, 0], s["got"][turn, t, 1]]
        top = functools.reduce(jnp.maximum, terms)
        total = functools.reduce(jnp.add, [jnp.exp2(a - top) for a in terms])
        g = (top + jnp.log2(total)) * (-shrink)
        s["dual"][t] = s["coord"][t][3] + g
        if turn == ITERS - 1:
            own = g[OWN] * (1.0 / unit)
            for q in range(blk):
                pot_ref[t : t + 1, q * BLOCK : (q + 1) * BLOCK] = own[q : q + 1]

    def pull(t):
        first, last = t == 0, t == group - 1
        acc = s["acc"]

        def body(p, _):
            where = [window_row(t, p, k) for k in range(pairs)]
            scale, y = [], []
            for k in range(pairs):
                scale.append(jnp.exp2(s["tops"][t, p, k : k + 1] + s["dual"][t, pl.ds(where[k], 1), :]))
                y.append([s["coord"][t][c, pl.ds(where[k], 1), :] for c in range(3)])
            parts = []
            for r in range(0, BLOCK, 32):
                sums = [None] * 4 if first else [acc[p, c, r : r + 32] for c in range(4)]
                for k in range(pairs):
                    plan = s["cost"][t, p, k, r : r + 32] * scale[k]
                    new = [plan * y[k][c] for c in range(3)] + [plan]
                    sums = [b if a is None else a + b for a, b in zip(sums, new)]
                if last:
                    parts.append([s["xcol"][c, p, r : r + 32] * sums[3] - sums[c] for c in range(3)])
                else:
                    for c in range(4):
                        acc[p, c, r : r + 32] = sums[c]
            if last:
                for c in range(3):
                    whole = jnp.transpose(jnp.concatenate([a[c] for a in parts], axis=0))
                    s["grad"][pl.ds(c * ROWS + p, 1), :] = jnp.sum(whole, axis=0, keepdims=True)
            return 0

        lax.fori_loop(0, blk, body, 0, unroll=2)

    for turn in range(ITERS):
        for t in range(group):
            if turn == 0:
                wait_recv(coord_copies(t))
            else:
                settle(turn - 1, t)
            sweep(turn, t)

    s["grad"][...] = jnp.zeros(s["grad"].shape, jnp.float32)
    for t in range(group):
        settle(ITERS - 1, t)
        pull(t)

    near = remote(s["grad"], s["grad_near"], s["n_send"], s["n_recv"], sibling)
    near.start()
    for t in range(group):
        wait_send(coord_copies(t))
        for turn in range(ITERS):
            wait_send(part_copies(turn, t))
    near.wait_recv()
    s["grad_far"][chip] = s["grad"][...] + s["grad_near"][...]

    def far(step, slot):
        return remote(
            s["grad_far"].at[chip], s["grad_far"].at[slot], s["f_send"].at[step - 1], s["f_recv"].at[slot],
            same_core(step),
        )

    for step in range(1, chips):
        far(step, chip).start()
    for step in range(1, chips):
        far(step, lax.rem(chip + step, chips)).wait_recv()
    total = s["grad_far"][0]
    for q in range(1, chips):
        total = total + s["grad_far"][q]
    for c in range(3):
        for q in range(blk):
            grad_ref[c : c + 1, q * BLOCK : (q + 1) * BLOCK] = total[c * ROWS + q : c * ROWS + q + 1]
    near.wait_send()
    for step in range(1, chips):
        far(step, chip).wait_send()


def shards(template_points, template_mass, target_points, target_mass, pattern):
    group, blk, pairs = pattern.shape
    width = blk * BLOCK
    count = lax.axis_size("pts")
    peers = lax.axis_size("tgt")
    f32 = jnp.float32

    names = {
        "coord": [pltpu.VMEM((4, SPAN, BLOCK), f32) for _ in range(group)],
        "dual": pltpu.VMEM((group, SPAN, BLOCK), f32),
        "part": pltpu.VMEM((ITERS, group, SPAN, BLOCK), f32),
        "got": pltpu.VMEM((ITERS, group, 2, SPAN, BLOCK), f32),
        "cost": pltpu.VMEM((group, blk, pairs, BLOCK, BLOCK), f32),
        "xcol": pltpu.VMEM((3, blk, BLOCK, BLOCK), f32),
        "acol": pltpu.VMEM((blk, BLOCK, BLOCK), f32),
        "tops": pltpu.VMEM((group, blk, 8, BLOCK), f32),
        "picked": pltpu.VMEM((blk, SPAN, BLOCK), f32),
        "best": pltpu.VMEM((SPAN, BLOCK), f32),
        "acc": pltpu.VMEM((blk, 4, BLOCK, BLOCK), f32),
        "grad": pltpu.VMEM((SPAN, BLOCK), f32),
        "grad_near": pltpu.VMEM((SPAN, BLOCK), f32),
        "grad_far": pltpu.VMEM((peers // CORES, SPAN, BLOCK), f32),
        "c_send": pltpu.SemaphoreType.DMA((group, 2)),
        "c_recv": pltpu.SemaphoreType.DMA((group, 2)),
        "p_send": pltpu.SemaphoreType.DMA((ITERS, group, 4)),
        "p_recv": pltpu.SemaphoreType.DMA((ITERS, group, 4)),
        "n_send": pltpu.SemaphoreType.DMA,
        "n_recv": pltpu.SemaphoreType.DMA,
        "f_send": pltpu.SemaphoreType.DMA((peers // CORES,)),
        "f_recv": pltpu.SemaphoreType.DMA((peers // CORES,)),
    }
    flat, tree = jax.tree.flatten(names)

    def run(*refs):
        kernel(group, blk, pairs, count, peers, refs[:5], refs[5:7], jax.tree.unflatten(tree, refs[7:]))

    whole = pl.BlockSpec(memory_space=pltpu.VMEM)
    elements = group * blk * pairs * BLOCK * BLOCK
    grad, pots = pl.pallas_call(
        run,
        out_shape=(
            jax.ShapeDtypeStruct((3, width), f32),
            jax.ShapeDtypeStruct((group, width), f32),
        ),
        in_specs=[whole, whole, whole, whole, pl.BlockSpec(memory_space=pltpu.SMEM)],
        out_specs=(whole, whole),
        scratch_shapes=flat,
        compiler_params=pltpu.CompilerParams(
            collective_id=0, has_side_effects=True, vmem_limit_bytes=48 * 1024 * 1024
        ),
        cost_estimate=pl.CostEstimate(
            flops=40 * elements, bytes_accessed=200000, transcendentals=6 * elements
        ),
        name="sinkhorn",
    )(
        template_points,
        template_mass.reshape(1, width),
        target_points.transpose(1, 0, 2),
        target_mass,
        pattern.transpose(0, 2, 1),
    )
    return grad, pots


def solution(mesh):
    placed = (
        P(None, "pts"),
        P("pts"),
        P("tgt", None, "pts"),
        P("tgt", "pts"),
        P("tgt", "pts", None),
    )
    return jax.shard_map(
        shards,
        mesh=mesh,
        in_specs=placed,
        out_specs=(P(None, "pts"), P("tgt", "pts")),
        check_vma=False,
    )
```

time: 89.5 us -> 62.4 us (0.70)
  Pallas kernels: 85.6 us -> 57.1 us
  local copies, waits for them, and re-layouts: 3.02 us -> 4.29 us
    pallas_call x1, Pallas kernels: 85.6 us -> 57.1 us  [shards(): pl.pallas_call(run, out_shape=(jax.ShapeDtypeStruct((3, width), f32), jax...]
    unnamed x12 -> x10, local copies, waits for them, and re-layouts: 2.31 us -> 3.58 us
where the time goes in v2:
time: 62.4 us; the launch traced here: 62 us
  Pallas kernels  57.1 us (92%)
  local copies, waits for them, and re-layouts  4.29 us (7%)
  between operations  0.65 us (1%)
    pallas_call x1, Pallas kernels, shards(): pl.pallas_call(run, out_shape=(jax.ShapeDtypeStruct((3, width), f32), jax...  57.1 us
    unnamed x10, local copies, waits for them, and re-layouts  3.58 us

profile of v2, /device:TPU:1, one launch (start us, length us, event | category | flops | bytes accessed | tf_op | source)
XLA Modules:
  0.0 62.0 jit_solution(5267774706451296296)
XLA Ops:
  0.6 0.0 copy-start.3
  0.6 0.7 %reshape.7.refs_1_ = f32[1,1536]{1,0:T(1,128)S(1)} reshape(f32[1536]{0:T(1024)} %param.6) | data formatting | bytes 12288 | tf_op jit(solution)/shard_map/reshape | solution.py:316
  1.3 0.0 copy-done.3
  1.4 0.0 copy-start
  1.4 0.9 %copy-done = f32[4,3,1536]{2,0,1:T(4,128)S(1)} copy-done((f32[4,3,1536]{2,0,1:T(4,128)S(1)}, f32[4,3,1536]{2,0,1:T(4,128)}, u32[]{:S(2)}) %copy-start) | copy-done | bytes 73752
  2.2 0.0 copy-start.1
  2.2 0.7 %copy-done.1 = f32[3,1536]{1,0:T(4,128)S(1)} copy-done((f32[3,1536]{1,0:T(4,128)S(1)}, f32[3,1536]{1,0:T(4,128)}, u32[]{:S(2)}) %copy-start.1) | copy-done | bytes 18456
  3.0 0.0 copy-start.2
  3.0 0.7 %copy-done.2 = f32[4,1536]{1,0:T(4,128)S(1)} copy-done((f32[4,1536]{1,0:T(4,128)S(1)}, f32[4,1536]{1,0:T(4,128)}, u32[]{:S(2)}) %copy-start.2) | copy-done | bytes 24600
  3.7 57.1 %sinkhorn.1 = (f32[3,1536]{1,0:T(4,128)S(1)}, f32[4,1536]{1,0:T(4,128)S(1)}) custom-call(f32[3,1536]{1,0:T(4,128)S(1)} %copy-done.1, f32[1,1536]{1,0:T(1,128)S(1)} %reshape.7.refs_1_, f32[3,4,1536]{2,1,0:T(4,128)S(1)} %bitcast.2, f32[4,1536]{1,0:T(4,128)S(1)} %copy-done.2, s32[4,4,12]{2,1,0:T(4,128)S(1)} %bitcast.3), custom_call_target="tpu_custom_call" | custom-call | flops 125829120 | bytes 200000 | tf_op jit(solution)/shard_map/sinkhorn/pallas_call | solution.py:298
  60.8 0.6 copy.9
  61.4 0.6 copy.10
Async XLA Ops:
  0.6 0.7 %copy-start.3 = (s32[4,12,4]{1,2,0:T(4,128)S(1)}, s32[4,12,4]{1,2,0:T(4,128)}, u32[]{:S(2)}) copy-start(s32[4,12,4]{1,2,0:T(4,128)} %param.9) | copy-start | bytes 2308
  1.4 0.9 %copy-start = (f32[4,3,1536]{2,0,1:T(4,128)S(1)}, f32[4,3,1536]{2,0,1:T(4,128)}, u32[]{:S(2)}) copy-start(f32[4,3,1536]{2,0,1:T(4,128)} %param.7) | copy-start | bytes 221188
  2.2 0.7 %copy-start.1 = (f32[3,1536]{1,0:T(4,128)S(1)}, f32[3,1536]{1,0:T(4,128)}, u32[]{:S(2)}) copy-start(f32[3,1536]{1,0:T(4,128)} %refs_0_.1) | copy-start | bytes 55300
  3.0 0.7 %copy-start.2 = (f32[4,1536]{1,0:T(4,128)S(1)}, f32[4,1536]{1,0:T(4,128)}, u32[]{:S(2)}) copy-start(f32[4,1536]{1,0:T(4,128)} %refs_3_.1) | copy-start | bytes 73732

commit v3 on v2

--- a/solution.py
+++ b/solution.py
@@ -26,9 +26,14 @@
 
 
 def kernel(group, blk, pairs, count, peers, refs, outs, scratch):
-    xp_ref, xm_ref, yp_ref, ym_ref, links_ref = refs
     grad_ref, pot_ref = outs
     s = scratch
+    held = ["yp", "ym", "xp", "xm", "links"]
+    order = [2, 3, 0, 1, 4]
+    loads = [
+        pltpu.make_async_copy(refs[order[i]], s[name], s["l_sem"].at[i]) for i, name in enumerate(held)
+    ]
+    xp_ref, xm_ref, yp_ref, ym_ref, links_ref = (s[name] for name in ("xp", "xm", "yp", "ym", "links"))
     me = lax.axis_index("pts")
     mine = lax.axis_index("tgt")
     chips = peers // CORES
@@ -86,11 +91,17 @@
         for c in copies:
             c.wait_recv()
 
+    for load in loads:
+        load.start()
+    loads[0].wait()
+    loads[1].wait()
     for t in range(group):
         for q in range(blk):
             lanes = slice(q * BLOCK, (q + 1) * BLOCK)
             for c in range(3):
-                s["coord"][t][c, ROWS + q : ROWS + q + 1] = yp_ref[c, t : t + 1, lanes]
+                row = yp_ref[c, t : t + 1, lanes]
+                s["coord"][t][c, ROWS + q : ROWS + q + 1] = row
+                s["own"][t, c, q : q + 1] = row
             s["coord"][t][3, ROWS + q : ROWS + q + 1] = jnp.log2(ym_ref[t : t + 1, lanes])
         for c in range(4):
             s["coord"][t][c, ROWS + blk : 2 * ROWS] = jnp.zeros((ROWS - blk, BLOCK), jnp.float32)
@@ -98,17 +109,38 @@
     pl.semaphore_wait(barrier, len(greeted))
     for t in range(group):
         start(coord_copies(t))
+
+    for load in loads[2:]:
+        load.wait()
 
     def columns(p, _):
         lanes = pl.ds(pl.multiple_of(p * BLOCK, BLOCK), BLOCK)
         for c in range(3):
             row = xp_ref[c : c + 1, lanes]
             s["xcol"][c, p] = jnp.transpose(jnp.broadcast_to(row, (BLOCK, BLOCK)))
-        row = jnp.log2(xm_ref[:, lanes])
+        row = jnp.log2(xm_ref[lanes]).reshape(1, BLOCK)
         s["acol"][p] = jnp.transpose(jnp.broadcast_to(row, (BLOCK, BLOCK)))
         return 0
 
     lax.fori_loop(0, blk, columns, 0, unroll=2)
+
+    def tile_cost(t, p, k, w):
+        y = [s["coord"][t][c, pl.ds(w, 1), :] for c in range(3)]
+        for r in range(0, BLOCK, 32):
+            d = [s["xcol"][c, p, r : r + 32] - y[c] for c in range(3)]
+            total = d[0] * d[0] + d[1] * d[1] + d[2] * d[2]
+            s["cost"][t, p, k, r : r + 32] = total * (0.5 * unit)
+
+    def own_tiles(p, _):
+        for t in range(group):
+            for r in range(0, BLOCK, 32):
+                y = [s["own"][t, c, pl.ds(p, 1), :] for c in range(3)]
+                d = [s["xcol"][c, p, r : r + 32] - y[c] for c in range(3)]
+                total = d[0] * d[0] + d[1] * d[1] + d[2] * d[2]
+                s["cost"][t, p, 0, r : r + 32] = total * (0.5 * unit)
+        return 0
+
+    lax.fori_loop(0, blk, own_tiles, 0)
 
     rows_iota = lax.broadcasted_iota(jnp.int32, (SPAN, BLOCK), 0)
 
@@ -127,19 +159,18 @@
             where = [window_row(t, p, k) for k in range(pairs)]
             if first:
                 duals = [s["coord"][t][3, pl.ds(w, 1), :] for w in where]
-                for k in range(pairs):
-                    y = [s["coord"][t][c, pl.ds(where[k], 1), :] for c in range(3)]
-                    for r in range(0, BLOCK, 32):
-                        d = [s["xcol"][c, p, r : r + 32] - y[c] for c in range(3)]
-                        total = d[0] * d[0] + d[1] * d[1] + d[2] * d[2]
-                        cost[t, p, k, r : r + 32] = total * (0.5 * unit)
+                for k in range(1, pairs):
+                    tile_cost(t, p, k, where[k])
             else:
                 duals = [s["dual"][t, pl.ds(w, 1), :] for w in where]
             heads = []
             for r in range(0, BLOCK, 32):
-                args = [duals[k] - cost[t, p, k, r : r + 32] for k in range(pairs)]
-                top = functools.reduce(jnp.maximum, args)
-                top = jnp.max(top, axis=1, keepdims=True)
+                costs = [cost[t, p, k, r : r + 32] for k in range(pairs)]
+                args = [duals[k] - costs[k] for k in range(pairs)]
+                if first:
+                    top = -jnp.min(functools.reduce(jnp.minimum, costs), axis=1, keepdims=True)
+                else:
+                    top = jnp.max(functools.reduce(jnp.maximum, args), axis=1, keepdims=True)
                 total = functools.reduce(jnp.add, [jnp.exp2(a - top) for a in args])
                 total = jnp.sum(total, axis=1, keepdims=True)
                 f = (top + jnp.log2(total)) * (-shrink)
@@ -265,6 +296,13 @@
     f32 = jnp.float32
 
     names = {
+        "xp": pltpu.VMEM((3, width), f32),
+        "xm": pltpu.VMEM((width,), f32),
+        "yp": pltpu.VMEM((3, group, width), f32),
+        "ym": pltpu.VMEM((group, width), f32),
+        "links": pltpu.SMEM((group, pairs, blk), jnp.int32),
+        "l_sem": pltpu.SemaphoreType.DMA((5,)),
+        "own": pltpu.VMEM((group, 3, ROWS, BLOCK), f32),
         "coord": [pltpu.VMEM((4, SPAN, BLOCK), f32) for _ in range(group)],
         "dual": pltpu.VMEM((group, SPAN, BLOCK), f32),
         "part": pltpu.VMEM((ITERS, group, SPAN, BLOCK), f32),
@@ -294,6 +332,7 @@
         kernel(group, blk, pairs, count, peers, refs[:5], refs[5:7], jax.tree.unflatten(tree, refs[7:]))
 
     whole = pl.BlockSpec(memory_space=pltpu.VMEM)
+    held = pl.BlockSpec(memory_space=pltpu.HBM)
     elements = group * blk * pairs * BLOCK * BLOCK
     grad, pots = pl.pallas_call(
         run,
@@ -301,11 +340,11 @@
             jax.ShapeDtypeStruct((3, width), f32),
             jax.ShapeDtypeStruct((group, width), f32),
         ),
-        in_specs=[whole, whole, whole, whole, pl.BlockSpec(memory_space=pltpu.SMEM)],
+        in_specs=[held] * 5,
         out_specs=(whole, whole),
         scratch_shapes=flat,
         compiler_params=pltpu.CompilerParams(
-            collective_id=0, has_side_effects=True, vmem_limit_bytes=48 * 1024 * 1024
+            collective_id=0, has_side_effects=True, vmem_limit_bytes=63 * 1024 * 1024
         ),
         cost_estimate=pl.CostEstimate(
             flops=40 * elements, bytes_accessed=200000, transcendentals=6 * elements
@@ -313,7 +352,7 @@
         name="sinkhorn",
     )(
         template_points,
-        template_mass.reshape(1, width),
+        template_mass,
         target_points.transpose(1, 0, 2),
         target_mass,
         pattern.transpose(0, 2, 1),

time: 62.4 us -> 58.9 us (0.944)
  local copies, waits for them, and re-layouts: 4.29 us -> 1.97 us
  Pallas kernels: 57.1 us -> 56.1 us
    unnamed x10 -> x4, local copies, waits for them, and re-layouts: 3.58 us -> 1.97 us
    pallas_call x1, Pallas kernels: 57.1 us -> 56.1 us  [shards(): pl.pallas_call(run, out_shape=(jax.ShapeDtypeStruct((3, width), f32), jax...]
    reshape x1 -> x0, local copies, waits for them, and re-layouts: 0.71 us -> none  [shards(): template_mass.reshape(1, width)]
where the time goes in v3:
time: 58.9 us; the launch traced here: 58.7 us
  Pallas kernels  56.1 us (95%)
  local copies, waits for them, and re-layouts  1.97 us (3%)
  between operations  0.65 us (1%)
    pallas_call x1, Pallas kernels, shards(): pl.pallas_call(run, out_shape=(jax.ShapeDtypeStruct((3, width), f32), jax...  56.1 us
    unnamed x4, local copies, waits for them, and re-layouts  1.97 us

profile of v3, /device:TPU:1, one launch (start us, length us, event | category | flops | bytes accessed | tf_op | source)
XLA Modules:
  0.0 58.7 jit_solution(11067972403474625414)
XLA Ops:
  0.6 56.1 %sinkhorn.1 = (f32[3,1536]{1,0:T(4,128)}, f32[4,1536]{1,0:T(4,128)}) custom-call(f32[3,1536]{1,0:T(4,128)} %refs_0_.1, f32[1536]{0:T(1024)} %refs_1_.1, f32[3,4,1536]{2,1,0:T(4,128)} %bitcast.2, f32[4,1536]{1,0:T(4,128)} %refs_3_.1, s32[4,4,12]{2,1,0:T(4,128)} %bitcast.3), custom_call_target="tpu_custom_call" | custom-call | flops 125829120 | bytes 200000 | tf_op jit(solution)/shard_map/sinkhorn/pallas_call | solution.py:337
  56.7 0.0 copy-start
  56.8 1.4 %copy.9 = f32[3,1536]{1,0:T(4,128)} copy(f32[3,1536]{1,0:T(4,128)} %get-tuple-element.4) | data formatting | bytes 36864
  58.1 0.0 copy-done
  58.1 0.6 %copy.10 = f32[4,1536]{1,0:T(4,128)} copy(f32[4,1536]{1,0:T(4,128)S(1)} %copy-done) | data formatting | bytes 49152
Async XLA Ops:
  56.7 1.4 %copy-start = (f32[4,1536]{1,0:T(4,128)S(1)}, f32[4,1536]{1,0:T(4,128)}, u32[]{:S(2)}) copy-start(f32[4,1536]{1,0:T(4,128)} %get-tuple-element.5) | copy-start | bytes 73732

commit v4 on v3

--- a/solution.py
+++ b/solution.py
@@ -107,8 +107,7 @@
             s["coord"][t][c, ROWS + blk : 2 * ROWS] = jnp.zeros((ROWS - blk, BLOCK), jnp.float32)
 
     pl.semaphore_wait(barrier, len(greeted))
-    for t in range(group):
-        start(coord_copies(t))
+    start(coord_copies(0))
 
     for load in loads[2:]:
         load.wait()
@@ -123,6 +122,8 @@
         return 0
 
     lax.fori_loop(0, blk, columns, 0, unroll=2)
+    if group > 1:
+        start(coord_copies(1))
 
     def tile_cost(t, p, k, w):
         y = [s["coord"][t][c, pl.ds(w, 1), :] for c in range(3)]
@@ -141,6 +142,8 @@
         return 0
 
     lax.fori_loop(0, blk, own_tiles, 0)
+    for t in range(2, group):
+        start(coord_copies(t))
 
     rows_iota = lax.broadcasted_iota(jnp.int32, (SPAN, BLOCK), 0)
 

time: 58.9 us -> 58.9 us (level)
  no operation moved by 1% of the time
where the time goes in v4:
time: 58.9 us; the launch traced here: 58.7 us
  Pallas kernels  56.1 us (95%)
  local copies, waits for them, and re-layouts  1.97 us (3%)
  between operations  0.65 us (1%)
    pallas_call x1, Pallas kernels, shards(): pl.pallas_call(run, out_shape=(jax.ShapeDtypeStruct((3, width), f32), jax...  56.1 us
    unnamed x4, local copies, waits for them, and re-layouts  1.97 us

profile of v4, /device:TPU:1, one launch (start us, length us, event | category | flops | bytes accessed | tf_op | source)
XLA Modules:
  0.0 58.7 jit_solution(15794910160482695971)
XLA Ops:
  0.6 56.1 %sinkhorn.1 = (f32[3,1536]{1,0:T(4,128)}, f32[4,1536]{1,0:T(4,128)}) custom-call(f32[3,1536]{1,0:T(4,128)} %refs_0_.1, f32[1536]{0:T(1024)} %refs_1_.1, f32[3,4,1536]{2,1,0:T(4,128)} %bitcast.2, f32[4,1536]{1,0:T(4,128)} %refs_3_.1, s32[4,4,12]{2,1,0:T(4,128)} %bitcast.3), custom_call_target="tpu_custom_call" | custom-call | flops 125829120 | bytes 200000 | tf_op jit(solution)/shard_map/sinkhorn/pallas_call | solution.py:340
  56.7 0.0 copy-start
  56.7 1.4 %copy.9 = f32[3,1536]{1,0:T(4,128)} copy(f32[3,1536]{1,0:T(4,128)} %get-tuple-element.4) | data formatting | bytes 36864
  58.1 0.0 copy-done
  58.1 0.6 %copy.10 = f32[4,1536]{1,0:T(4,128)} copy(f32[4,1536]{1,0:T(4,128)S(1)} %copy-done) | data formatting | bytes 49152
Async XLA Ops:
  56.7 1.4 %copy-start = (f32[4,1536]{1,0:T(4,128)S(1)}, f32[4,1536]{1,0:T(4,128)}, u32[]{:S(2)}) copy-start(f32[4,1536]{1,0:T(4,128)} %get-tuple-element.5) | copy-start | bytes 73732

commit v5 on v3

--- a/solution.py
+++ b/solution.py
@@ -193,7 +193,7 @@
             return 0
 
         s["best"][...] = jnp.full((SPAN, BLOCK), lowest, jnp.float32)
-        lax.fori_loop(0, blk, body, 0, unroll=4)
+        lax.fori_loop(0, blk, body, 0, unroll=6)
         best = s["best"][...]
 
         def add(p, total):
@@ -243,7 +243,7 @@
                     s["grad"][pl.ds(c * ROWS + p, 1), :] = jnp.sum(whole, axis=0, keepdims=True)
             return 0
 
-        lax.fori_loop(0, blk, body, 0, unroll=2)
+        lax.fori_loop(0, blk, body, 0, unroll=4)
 
     for turn in range(ITERS):
         for t in range(group):

time: 58.9 us -> 58.6 us (level)
  no operation moved by 1% of the time
where the time goes in v5:
time: 58.6 us; the launch traced here: 58.4 us
  Pallas kernels  55.8 us (95%)
  local copies, waits for them, and re-layouts  1.97 us (3%)
  between operations  0.65 us (1%)
    pallas_call x1, Pallas kernels, shards(): pl.pallas_call(run, out_shape=(jax.ShapeDtypeStruct((3, width), f32), jax...  55.8 us
    unnamed x4, local copies, waits for them, and re-layouts  1.97 us

profile of v5, /device:TPU:1, one launch (start us, length us, event | category | flops | bytes accessed | tf_op | source)
XLA Modules:
  0.0 58.4 jit_solution(15123194096734869083)
XLA Ops:
  0.6 55.8 %sinkhorn.1 = (f32[3,1536]{1,0:T(4,128)}, f32[4,1536]{1,0:T(4,128)}) custom-call(f32[3,1536]{1,0:T(4,128)} %refs_0_.1, f32[1536]{0:T(1024)} %refs_1_.1, f32[3,4,1536]{2,1,0:T(4,128)} %bitcast.2, f32[4,1536]{1,0:T(4,128)} %refs_3_.1, s32[4,4,12]{2,1,0:T(4,128)} %bitcast.3), custom_call_target="tpu_custom_call" | custom-call | flops 125829120 | bytes 200000 | tf_op jit(solution)/shard_map/sinkhorn/pallas_call | solution.py:337
  56.4 0.0 copy-start
  56.4 1.4 %copy.9 = f32[3,1536]{1,0:T(4,128)} copy(f32[3,1536]{1,0:T(4,128)} %get-tuple-element.4) | data formatting | bytes 36864
  57.8 0.0 copy-done
  57.8 0.6 %copy.10 = f32[4,1536]{1,0:T(4,128)} copy(f32[4,1536]{1,0:T(4,128)S(1)} %copy-done) | data formatting | bytes 49152
Async XLA Ops:
  56.4 1.4 %copy-start = (f32[4,1536]{1,0:T(4,128)S(1)}, f32[4,1536]{1,0:T(4,128)}, u32[]{:S(2)}) copy-start(f32[4,1536]{1,0:T(4,128)} %get-tuple-element.5) | copy-start | bytes 73732
